TPU v7x, 32 devices: a whole 2x2x4 slice. The times are simulated.
32 devices in a mesh: expert: 8 (over z, y), hidden: 4 (over x, core).
Axes of the slice: x: 2, y: 2, z: 4, core: 2. Of those that a mesh axis runs over, the one named last changes fastest.
Arguments:
- tokens: bfloat16 [4096, 2048], P(('expert', 'hidden')), may hold values from -6 to 6
- grad_out: bfloat16 [4096, 2048], P(('expert', 'hidden')), may hold values from -6 to 6
- picks: int32 [16, 512], P('expert'), may hold values from 0 to 4095, as said below
- gates: float32 [16, 512], P('expert'), may hold values from 0.1 to 1
- w_gate: bfloat16 [16, 768, 2048], P('expert', 'hidden'), may hold values from -0.125 to 0.125
- w_up: bfloat16 [16, 768, 2048], P('expert', 'hidden'), may hold values from -0.125 to 0.125
- w_down: bfloat16 [16, 768, 2048], P('expert', 'hidden'), may hold values from -0.21875 to 0.21875
Outputs:
- grad_tokens: bfloat16 [4096, 2048], P(('expert', 'hidden'))
- grad_scores: float32 [16, 512], P('expert')
- grad_w_gate: bfloat16 [16, 768, 2048], P('expert', 'hidden')
- grad_w_up: bfloat16 [16, 768, 2048], P('expert', 'hidden')
- grad_w_down: bfloat16 [16, 768, 2048], P('expert', 'hidden')
Inputs may be any that keep to these rules, and one draw needn't show every extreme that they name: Each row lists 512 different token indices in ascending order. For every expert at most 32 of its picks lie in one aligned block of 128 tokens, and some block holds exactly 32.
All inputs are finite; a program needn't handle non-finite values.
Results may differ from a plain program's by a relative error of at most 0.01.
Values may be sent and summed in bfloat16 or wider, within the bound.
A program may use at most 128 MiB of HBM per device.

v0:
```python
import jax
import jax.numpy as jnp
from jax import lax
from jax.sharding import PartitionSpec as P


def local(tokens, grad_out, picks, gates, w_gate, w_up, w_down):
    groups = lax.axis_size("expert")
    shares = lax.axis_size("hidden")
    tok_rows, width = tokens.shape
    exp_local, capacity = picks.shape
    most = 2 * capacity // (groups * shares)
    all_picks = lax.all_gather(picks, "expert", axis=0, tiled=True)
    owner = lax.axis_index("expert") * shares + lax.axis_index("hidden")
    base = owner * tok_rows
    starts = jax.vmap(lambda row: jnp.searchsorted(row, base))(all_picks)
    ends = jax.vmap(lambda row: jnp.searchsorted(row, base + tok_rows))(all_picks)
    position = starts[:, None] + jnp.arange(most, dtype=jnp.int32)[None, :]
    valid = position < ends[:, None]
    local_rows = jnp.take_along_axis(all_picks, jnp.minimum(position, capacity - 1), axis=1) - base
    local_rows = jnp.where(valid, local_rows, 0).reshape(-1)
    valid_rows = valid.reshape(-1)[:, None]
    send_rows = jnp.where(valid_rows, tokens[local_rows], jnp.zeros((), jnp.bfloat16)).reshape(
        groups, exp_local, most, width
    )
    send_grads = jnp.where(valid_rows, grad_out[local_rows], jnp.zeros((), jnp.bfloat16)).reshape(
        groups, exp_local, most, width
    )
    got_rows, got_grads = (
        lax.all_to_all(send_rows, "expert", split_axis=0, concat_axis=0, tiled=True),
        lax.all_to_all(send_grads, "expert", split_axis=0, concat_axis=0, tiled=True),
    )
    rows_all, grads_all = (
        lax.all_gather(got_rows[None], "hidden", axis=0, tiled=True),
        lax.all_gather(got_grads[None], "hidden", axis=0, tiled=True),
    )
    source = picks // tok_rows
    first = jax.vmap(jnp.searchsorted)(picks, source * tok_rows)
    rank = jnp.arange(capacity, dtype=jnp.int32)[None, :] - first
    slot_index = (
        (source % shares * groups + source // shares) * exp_local
        + jnp.arange(exp_local, dtype=jnp.int32)[:, None]
    ) * most + rank
    flat_index = slot_index.reshape(-1)
    picked = rows_all.reshape(-1, width)[flat_index].reshape(exp_local, capacity, width)
    picked_grad = grads_all.reshape(-1, width)[flat_index].reshape(exp_local, capacity, width)
    gate = jnp.einsum("xcd,xhd->xch", picked, w_gate, preferred_element_type=jnp.float32)
    up = jnp.einsum("xcd,xhd->xch", picked, w_up, preferred_element_type=jnp.float32)
    sig = jax.nn.sigmoid(gate)
    act = gate * sig
    hid = (act * up).astype(jnp.bfloat16)
    back = jnp.einsum("xcd,xhd->xch", picked_grad, w_down, preferred_element_type=jnp.float32)
    score_part = jnp.sum(hid.astype(jnp.float32) * back, axis=-1)
    grad_scores = lax.psum(score_part, "hidden")
    grad_hid = gates[:, :, None] * back
    grad_gate = (grad_hid * up * sig * (1.0 + gate * (1.0 - sig))).astype(jnp.bfloat16)
    grad_up = (grad_hid * act).astype(jnp.bfloat16)
    weighted = (gates[:, :, None] * hid.astype(jnp.float32)).astype(jnp.bfloat16)
    grad_w_down = jnp.einsum(
        "xch,xcd->xhd", weighted, picked_grad, preferred_element_type=jnp.float32
    ).astype(jnp.bfloat16)
    grad_w_gate = jnp.einsum(
        "xch,xcd->xhd", grad_gate, picked, preferred_element_type=jnp.float32
    ).astype(jnp.bfloat16)
    grad_w_up = jnp.einsum(
        "xch,xcd->xhd", grad_up, picked, preferred_element_type=jnp.float32
    ).astype(jnp.bfloat16)
    partial_rows = jnp.einsum(
        "xch,xhd->xcd", grad_gate, w_gate, preferred_element_type=jnp.float32
    ) + jnp.einsum("xch,xhd->xcd", grad_up, w_up, preferred_element_type=jnp.float32)
    holder = jnp.zeros((shares * groups * exp_local * most, width), jnp.bfloat16)
    holder = holder.at[flat_index].set(partial_rows.reshape(-1, width).astype(jnp.bfloat16))
    holder = holder.reshape(shares, groups, exp_local, most, width)
    summed = lax.psum_scatter(holder, "hidden", scatter_dimension=0, tiled=True).astype(jnp.float32)
    rows_grad = summed[0].astype(jnp.bfloat16)
    back_home = lax.all_to_all(rows_grad, "expert", split_axis=0, concat_axis=0, tiled=True)
    selector = (
        (local_rows[:, None] == jnp.arange(tok_rows, dtype=jnp.int32)[None, :]) & valid_rows
    ).astype(jnp.bfloat16)
    grad_tokens = jnp.einsum(
        "st,sd->td", selector, back_home.reshape(-1, width), preferred_element_type=jnp.float32
    ).astype(jnp.bfloat16)
    return (grad_tokens, grad_scores, grad_w_gate, grad_w_up, grad_w_down)


def solution(mesh):
    placed = (
        P(("expert", "hidden"), None),
        P(("expert", "hidden"), None),
        P("expert", None),
        P("expert", None),
        P("expert", "hidden", None),
        P("expert", "hidden", None),
        P("expert", "hidden", None),
    )
    return jax.shard_map(
        local,
        mesh=mesh,
        in_specs=placed,
        out_specs=(
            P(("expert", "hidden"), None),
            P("expert", None),
            P("expert", "hidden", None),
            P("expert", "hidden", None),
            P("expert", "hidden", None),
        ),
        check_vma=False,
    )
```

profile of v0, /device:TPU:0, one launch (start us, length us, event | category | flops | bytes accessed | tf_op | source)
XLA Modules:
  0.0 446.3 jit_solution(7804300274067037993)
XLA Ops:
  7.3 32.5 %all-gather.2 = s32[8,2,512]{2,1,0:T(2,128)S(1)} all-gather(s32[1,2,512]{2,1,0:T(2,128)} %bitcast.80), channel_id=1, replica_groups=mesh['expert'=8,'hidden'=4] {'expert'}, dimensions={0}, use_global_device_ids=true | all-gather | bytes 36864 | tf_op jit(solution)/shard_map/all_gather | solution.py:13
  39.8 7.3 %while.58 = (s32[]{:T(128)}, u32[16]{0:T(128)S(1)}, u32[16]{0:T(128)S(1)}, s32[]{:T(128)}, s32[16,512]{1,0:T(8,128)S(1)}, /*index=5*/s32[]{:T(128)}, s32[]{:T(128)}) while((s32[]{:T(128)}, u32[16]{0:T(128)S(1)}, u32[16]{0:T(128)S(1)}, s32[]{:T(128)}, s32[16,512]{1,0:T(8,128)S(1)}, /*index=5*/s32[]{:T(128)}, s32[]{:T(128)}) %tuple.104), condition=%wide.region_1.2_spmd.clone, body=%wide.region_0.1_spmd.clone.sunk | while | flops 291 | bytes 860 | solution.py:16
  47.4 7.3 %while.59 = (s32[]{:T(128)}, u32[16]{0:T(128)S(1)}, u32[16]{0:T(128)S(1)}, s32[]{:T(128)}, s32[16,512]{1,0:T(8,128)S(1)}, /*index=5*/s32[]{:T(128)}, s32[]{:T(128)}) while((s32[]{:T(128)}, u32[16]{0:T(128)S(1)}, u32[16]{0:T(128)S(1)}, s32[]{:T(128)}, s32[16,512]{1,0:T(8,128)S(1)}, /*index=5*/s32[]{:T(128)}, s32[]{:T(128)}) %tuple.114), condition=%wide.region_3.4_spmd.clone, body=%wide.region_2.3_spmd.clone.sunk | while | flops 291 | bytes 860 | solution.py:17
  55.2 4.5 %gather_fusion.7 = s32[512]{0:T(512)S(1)} fusion(s32[16,512]{1,0:T(8,128)S(1)} %get-tuple-element.465, s32[512]{0:T(512)S(1)} %reshape.345), kind=kCustom, calls=%fused_computation.7 | custom fusion | bytes 8192 | tf_op jit(solution)/shard_map/jit(take_along_axis)/gather | solution.py:20
  70.4 47.3 %all_to_all.15 = bf16[8,2,32,2048]{3,2,1,0:T(8,128)(2,1)} all-to-all(bf16[8,2,32,2048]{3,2,1,0:T(8,128)(2,1)S(1)} %get-tuple-element.291), channel_id=1, replica_groups=mesh['expert'=8,'hidden'=4] {'expert'}, dimensions={0} | all-to-all | bytes 4194304 | tf_op jit(solution)/shard_map/all_to_all | solution.py:31
  117.7 49.6 %all_to_all.16 = bf16[8,2,32,2048]{3,2,1,0:T(8,128)(2,1)} all-to-all(bf16[8,2,32,2048]{3,2,1,0:T(8,128)(2,1)} %get-tuple-element.292), channel_id=1, replica_groups=mesh['expert'=8,'hidden'=4] {'expert'}, dimensions={0} | all-to-all | bytes 4194304 | tf_op jit(solution)/shard_map/all_to_all | solution.py:30
  167.4 92.3 %while.60 = (s32[]{:T(128)}, u32[2,512]{1,0:T(2,128)S(1)}, u32[2,512]{1,0:T(2,128)S(1)}, s32[2,512]{1,0:T(2,128)S(1)}, s32[2,512]{1,0:T(2,128)S(1)}, /*index=5*/s32[]{:T(128)}, s32[]{:T(128)}) while((s32[]{:T(128)}, u32[2,512]{1,0:T(2,128)S(1)}, u32[2,512]{1,0:T(2,128)S(1)}, s32[2,512]{1,0:T(2,128)S(1)}, s32[2,512]{1,0:T(2,128)S(1)}, ...), condition=%wide.region_5.6_spmd.clone, body=%wide.region_4.5_spmd.clone.sunk | while | flops 23555 | bytes 88153 | solution.py:38
  167.4 9.1 %gather_fusion.2 = s32[1024]{0:T(1024)S(1)} fusion(s32[2,512]{1,0:T(2,128)S(1)} %get-tuple-element.415, u32[1024]{0:T(1024)S(1)} %bitcast.81), kind=kCustom, calls=%fused_computation.2.clone.clone.1 | custom fusion | bytes 16384 | tf_op jit(solution)/shard_map/vmap(jit(searchsorted))/vmap(jit(_searchsorted_scan_impl))/while/body/eval_jaxpr/gather | solution.py:38
  176.7 9.1 %gather_fusion.2 = s32[1024]{0:T(1024)S(1)} fusion(s32[2,512]{1,0:T(2,128)S(1)} %get-tuple-element.415, u32[1024]{0:T(1024)S(1)} %bitcast.81), kind=kCustom, calls=%fused_computation.2.clone.clone.1 | custom fusion | bytes 16384 | tf_op jit(solution)/shard_map/vmap(jit(searchsorted))/vmap(jit(_searchsorted_scan_impl))/while/body/eval_jaxpr/gather | solution.py:38
  185.9 9.1 %gather_fusion.2 = s32[1024]{0:T(1024)S(1)} fusion(s32[2,512]{1,0:T(2,128)S(1)} %get-tuple-element.415, u32[1024]{0:T(1024)S(1)} %bitcast.81), kind=kCustom, calls=%fused_computation.2.clone.clone.1 | custom fusion | bytes 16384 | tf_op jit(solution)/shard_map/vmap(jit(searchsorted))/vmap(jit(_searchsorted_scan_impl))/while/body/eval_jaxpr/gather | solution.py:38
  195.1 9.1 %gather_fusion.2 = s32[1024]{0:T(1024)S(1)} fusion(s32[2,512]{1,0:T(2,128)S(1)} %get-tuple-element.415, u32[1024]{0:T(1024)S(1)} %bitcast.81), kind=kCustom, calls=%fused_computation.2.clone.clone.1 | custom fusion | bytes 16384 | tf_op jit(solution)/shard_map/vmap(jit(searchsorted))/vmap(jit(_searchsorted_scan_impl))/while/body/eval_jaxpr/gather | solution.py:38
  204.4 9.1 %gather_fusion.2 = s32[1024]{0:T(1024)S(1)} fusion(s32[2,512]{1,0:T(2,128)S(1)} %get-tuple-element.415, u32[1024]{0:T(1024)S(1)} %bitcast.81), kind=kCustom, calls=%fused_computation.2.clone.clone.1 | custom fusion | bytes 16384 | tf_op jit(solution)/shard_map/vmap(jit(searchsorted))/vmap(jit(_searchsorted_scan_impl))/while/body/eval_jaxpr/gather | solution.py:38
  213.6 9.1 %gather_fusion.2 = s32[1024]{0:T(1024)S(1)} fusion(s32[2,512]{1,0:T(2,128)S(1)} %get-tuple-element.415, u32[1024]{0:T(1024)S(1)} %bitcast.81), kind=kCustom, calls=%fused_computation.2.clone.clone.1 | custom fusion | bytes 16384 | tf_op jit(solution)/shard_map/vmap(jit(searchsorted))/vmap(jit(_searchsorted_scan_impl))/while/body/eval_jaxpr/gather | solution.py:38
  222.8 9.1 %gather_fusion.2 = s32[1024]{0:T(1024)S(1)} fusion(s32[2,512]{1,0:T(2,128)S(1)} %get-tuple-element.415, u32[1024]{0:T(1024)S(1)} %bitcast.81), kind=kCustom, calls=%fused_computation.2.clone.clone.1 | custom fusion | bytes 16384 | tf_op jit(solution)/shard_map/vmap(jit(searchsorted))/vmap(jit(_searchsorted_scan_impl))/while/body/eval_jaxpr/gather | solution.py:38
  232.1 9.1 %gather_fusion.2 = s32[1024]{0:T(1024)S(1)} fusion(s32[2,512]{1,0:T(2,128)S(1)} %get-tuple-element.415, u32[1024]{0:T(1024)S(1)} %bitcast.81), kind=kCustom, calls=%fused_computation.2.clone.clone.1 | custom fusion | bytes 16384 | tf_op jit(solution)/shard_map/vmap(jit(searchsorted))/vmap(jit(_searchsorted_scan_impl))/while/body/eval_jaxpr/gather | solution.py:38
  241.3 9.1 %gather_fusion.2 = s32[1024]{0:T(1024)S(1)} fusion(s32[2,512]{1,0:T(2,128)S(1)} %get-tuple-element.415, u32[1024]{0:T(1024)S(1)} %bitcast.81), kind=kCustom, calls=%fused_computation.2.clone.clone.1 | custom fusion | bytes 16384 | tf_op jit(solution)/shard_map/vmap(jit(searchsorted))/vmap(jit(_searchsorted_scan_impl))/while/body/eval_jaxpr/gather | solution.py:38
  250.5 9.1 %gather_fusion.2 = s32[1024]{0:T(1024)S(1)} fusion(s32[2,512]{1,0:T(2,128)S(1)} %get-tuple-element.415, u32[1024]{0:T(1024)S(1)} %bitcast.81), kind=kCustom, calls=%fused_computation.2.clone.clone.1 | custom fusion | bytes 16384 | tf_op jit(solution)/shard_map/vmap(jit(searchsorted))/vmap(jit(_searchsorted_scan_impl))/while/body/eval_jaxpr/gather | solution.py:38
  259.8 13.3 %gather_fusion.4 = bf16[1024,2048]{1,0:T(8,128)(2,1)} fusion(bf16[2048,2048]{1,0:T(8,128)(2,1)} %bitcast.82, s32[1024]{0:T(1024)S(1)} %broadcast_clamp_fusion), kind=kCustom, calls=%fused_computation.4 | custom fusion | bytes 8392704 | tf_op jit(solution)/shard_map/gather | solution.py:46
  273.1 13.3 %gather_fusion.6 = bf16[1024,2048]{1,0:T(8,128)(2,1)} fusion(bf16[2048,2048]{1,0:T(8,128)(2,1)} %bitcast.83, s32[1024]{0:T(1024)S(1)} %broadcast_clamp_fusion), kind=kCustom, calls=%fused_computation.6 | custom fusion | bytes 8392704 | tf_op jit(solution)/shard_map/gather | solution.py:45
  299.6 12.4 %scatter_custom_fusion = bf16[2048,2048]{1,0:T(8,128)(2,1)} fusion(s32[1024]{0:T(1024)S(1)} %bitcast.97, bf16[1024,2048]{1,0:T(8,128)(2,1)} %bitcast.93, bf16[]{:T(256)} %constant.143.clone.1), kind=kCustom, calls=%fused_computation.31 | custom fusion | bytes 8389120 | tf_op jit(solution)/shard_map/scatter | solution.py:72
  312.0 70.9 %reduce-scatter.2.cloned.1.call-done = bf16[1,8,2,32,2048]{4,3,2,1,0:T(8,128)(2,1)} async-done(((bf16[4,8,2,32,2048]{4,3,2,1,0:T(8,128)(2,1)}), bf16[1,8,2,32,2048]{4,3,2,1,0:T(8,128)(2,1)}) %reduce-scatter.2.cloned.1.call-update) | async-done | bytes 2097168 | tf_op jit(solution)/shard_map/reduce_scatter | solution.py:74
  382.9 5.5 %all-to-all-start.2 = ((bf16[8,2,32,2048]{3,2,1,0:T(8,128)(2,1)}), bf16[8,2,32,2048]{3,2,1,0:T(8,128)(2,1)}, u32[]{:S(2)}, u32[]{:S(2)}) async-start(bf16[8,2,32,2048]{3,2,1,0:T(8,128)(2,1)} %bitcast.94), calls=%async_computation.3 | async-start | bytes 4194304 | tf_op jit(solution)/shard_map/all_to_all | solution.py:76
  388.7 6.7 %psum.7 = f32[2,512]{1,0:T(2,128)} all-reduce(f32[2,512]{1,0:T(2,128)S(1)} %get-tuple-element.279), channel_id=1, replica_groups=mesh['expert'=8,'hidden'=4] {'hidden'}, use_global_device_ids=true, to_apply=%region_9.10 | all-reduce | flops 1024 | bytes 8192 | tf_op jit(solution)/shard_map/psum | solution.py:54
  404.8 31.9 %all-to-all-done.2 = bf16[8,2,32,2048]{3,2,1,0:T(8,128)(2,1)} async-done(((bf16[8,2,32,2048]{3,2,1,0:T(8,128)(2,1)}), bf16[8,2,32,2048]{3,2,1,0:T(8,128)(2,1)}, u32[]{:S(2)}, u32[]{:S(2)}) %all-to-all-start.2) | async-done | bytes 2097184 | tf_op jit(solution)/shard_map/all_to_all | solution.py:76
  (198 shorter events, 52.3 us)
Async XLA Ops:
  7.2 279.2 %copy-start = (bf16[2,192,2048]{2,1,0:T(8,128)(2,1)S(1)}, bf16[2,192,2048]{2,1,0:T(8,128)(2,1)}, u32[]{:S(2)}) copy-start(bf16[2,192,2048]{2,1,0:T(8,128)(2,1)} %param.17) | copy-start | bytes 4718596
  7.2 252.6 %all-gather.6.cloned.1.call-start = ((), (), s32[]{:S(2)}) async-start(), calls=%async_computation.5 | async-start | bytes 10485760 | tf_op jit(solution)/shard_map/all_gather | solution.py:35
  55.2 4.6 %copy-start.2 = (bf16[128,2048]{1,0:T(8,128)(2,1)S(1)}, bf16[128,2048]{1,0:T(8,128)(2,1)}, u32[]{:S(2)}) copy-start(bf16[128,2048]{1,0:T(8,128)(2,1)} %param.13) | copy-start | bytes 1572868
  59.8 3.3 copy-start.3
  117.7 155.4 %all-gather.8.cloned.1.call-start = ((), (), s32[]{:S(2)}) async-start(), calls=%async_computation.6 | async-start | bytes 10485760 | tf_op jit(solution)/shard_map/all_gather | solution.py:34
  117.7 49.7 %copy-start.1 = (s32[2,512]{1,0:T(2,128)S(1)}, s32[2,512]{1,0:T(2,128)}, u32[]{:S(2)}) copy-start(s32[2,512]{1,0:T(2,128)} %param.15) | copy-start | bytes 12292
  167.3 215.6 %reduce-scatter.2.cloned.1.call-start = ((), (), s32[]{:S(2)}) async-start(), calls=%async_computation.4 | async-start | bytes 10485760 | tf_op jit(solution)/shard_map/reduce_scatter | solution.py:74
  286.4 3.9 copy-start.4
  286.4 3.9 copy-start.8
  290.3 2.2 copy-start.6
  290.3 2.2 copy-start.9
  290.3 2.7 copy-start.10
  382.9 53.9 %all-to-all-start.2 = ((bf16[8,2,32,2048]{3,2,1,0:T(8,128)(2,1)}), bf16[8,2,32,2048]{3,2,1,0:T(8,128)(2,1)}, u32[]{:S(2)}, u32[]{:S(2)}) async-start(bf16[8,2,32,2048]{3,2,1,0:T(8,128)(2,1)} %bitcast.94), calls=%async_computation.3 | async-start | bytes 4194304 | tf_op jit(solution)/shard_map/all_to_all | solution.py:76
  395.4 4.5 %copy-start.5 = (bf16[1024,2048]{1,0:T(8,128)(2,1)S(1)}, bf16[1024,2048]{1,0:T(8,128)(2,1)}, u32[]{:S(2)}) copy-start(bf16[1024,2048]{1,0:T(8,128)(2,1)} %gather_fusion.6) | copy-start | bytes 12582916
  399.9 2.8 copy-start.7
Sparse Core Ops, SparseCore 0:
  117.8 57.2 all-gather.5
  176.7 58.2 all-gather.7
  312.1 70.7 reduce-scatter.1
where the time goes:
time: 447 us; the launch traced here: 446 us
  local copies, waits for them, and re-layouts  158 us (35%)
  blocking collectives  136 us (30%)
  waiting for transfers between devices  103 us (23%)
  matrix products  23.7 us (5%)
  between operations  14 us (3%)
  starting transfers between devices  5.64 us (1%)
  other arithmetic  5.12 us (1%)
    gather x10, local copies, waits for them, and re-layouts, local(): first = jax.vmap(jnp.searchsorted)(picks, source * tok_rows)  91.1 us
    reduce_scatter x1, waiting for transfers between devices, local(): lax.psum_scatter(holder, 'hidden', scatter_dimension=0, tiled=True)  70.9 us
    all_to_all x1, blocking collectives, local(): lax.all_to_all(send_rows, 'expert', split_axis=0, concat_axis=0, tiled=True)  49.6 us
    all_to_all x1, blocking collectives, local(): lax.all_to_all(send_grads, 'expert', split_axis=0, concat_axis=0, tiled=T...  47.3 us
    all_gather x1, blocking collectives, local(): all_picks = lax.all_gather(picks, 'expert', axis=0, tiled=True)  32.5 us
    all_to_all x1, waiting for transfers between devices, local(): lax.all_to_all(rows_grad, 'expert', split_axis=0, concat_axis=0, tiled=True)  31.9 us
    gather x20, local copies, waits for them, and re-layouts, local(): starts = jax.vmap(lambda row: jnp.searchsorted(row, base))(all_picks)  13.7 us
    gather x1, local copies, waits for them, and re-layouts, local(): rows_all.reshape(-1, width)[flat_index].reshape(exp_local, capacity, width)  13.3 us
  transfers between devices with their start and end apart: 4, of which 2 were waited for; matrix products, arithmetic and copies ran while one was open for 26% of the time, Pallas kernels for 0%

commit v1 on v0

v1 whole, which is shorter than its diff:
```python
import jax
import jax.numpy as jnp
from jax import lax
from jax.sharding import PartitionSpec as P


def local(tokens, grad_out, picks, gates, w_gate, w_up, w_down):
    groups = lax.axis_size("expert")
    shares = lax.axis_size("hidden")
    tok_rows, width = tokens.shape
    exp_local, capacity = picks.shape
    total = groups * shares * tok_rows
    cols = width // shares
    flat = picks.reshape(-1)

    def spread(rows):
        part = lax.all_to_all(rows, "hidden", split_axis=1, concat_axis=0, tiled=True)
        return lax.all_gather(part, "expert", axis=0, tiled=True)

    def collect(everything):
        mine = everything[flat]
        return lax.all_gather(mine, "hidden", axis=1, tiled=True).reshape(exp_local, capacity, width)

    picked_grad = collect(spread(grad_out))
    picked = collect(spread(tokens))
    back = jnp.einsum("xcd,xhd->xch", picked_grad, w_down, preferred_element_type=jnp.float32)
    gate = jnp.einsum("xcd,xhd->xch", picked, w_gate, preferred_element_type=jnp.float32)
    up = jnp.einsum("xcd,xhd->xch", picked, w_up, preferred_element_type=jnp.float32)
    sig = jax.nn.sigmoid(gate)
    act = gate * sig
    hid = (act * up).astype(jnp.bfloat16)
    score_part = jnp.sum(hid.astype(jnp.float32) * back, axis=-1)
    grad_scores = lax.psum(score_part, "hidden")
    grad_hid = gates[:, :, None] * back
    grad_gate = (grad_hid * up * sig * (1.0 + gate * (1.0 - sig))).astype(jnp.bfloat16)
    grad_up = (grad_hid * act).astype(jnp.bfloat16)
    weighted = (gates[:, :, None] * hid.astype(jnp.float32)).astype(jnp.bfloat16)
    partial_rows = (
        jnp.einsum("xch,xhd->xcd", grad_gate, w_gate, preferred_element_type=jnp.float32)
        + jnp.einsum("xch,xhd->xcd", grad_up, w_up, preferred_element_type=jnp.float32)
    ).astype(jnp.bfloat16)
    rows_grad = lax.psum_scatter(
        partial_rows.reshape(exp_local * capacity, width), "hidden", scatter_dimension=1, tiled=True
    )
    selector = (jnp.arange(total, dtype=jnp.int32)[:, None] == flat[None, :]).astype(jnp.bfloat16)
    sums = jnp.dot(selector, rows_grad, preferred_element_type=jnp.float32).astype(jnp.bfloat16)
    own = lax.psum_scatter(sums, "expert", scatter_dimension=0, tiled=True)
    grad_tokens = lax.all_to_all(own, "hidden", split_axis=0, concat_axis=1, tiled=True)
    grad_w_down = jnp.einsum(
        "xch,xcd->xhd", weighted, picked_grad, preferred_element_type=jnp.float32
    ).astype(jnp.bfloat16)
    grad_w_gate = jnp.einsum(
        "xch,xcd->xhd", grad_gate, picked, preferred_element_type=jnp.float32
    ).astype(jnp.bfloat16)
    grad_w_up = jnp.einsum(
        "xch,xcd->xhd", grad_up, picked, preferred_element_type=jnp.float32
    ).astype(jnp.bfloat16)
    return (grad_tokens, grad_scores, grad_w_gate, grad_w_up, grad_w_down)


def solution(mesh):
    placed = (
        P(("expert", "hidden"), None),
        P(("expert", "hidden"), None),
        P("expert", None),
        P("expert", None),
        P("expert", "hidden", None),
        P("expert", "hidden", None),
        P("expert", "hidden", None),
    )
    return jax.shard_map(
        local,
        mesh=mesh,
        in_specs=placed,
        out_specs=(
            P(("expert", "hidden"), None),
            P("expert", None),
            P("expert", "hidden", None),
            P("expert", "hidden", None),
            P("expert", "hidden", None),
        ),
        check_vma=False,
    )
```

time: 447 us -> 420 us (0.940)
  waiting for transfers between devices: 103 us -> 311 us
  local copies, waits for them, and re-layouts: 158 us -> 18.8 us
  blocking collectives: 136 us -> 32.8 us
  matrix products: 23.7 us -> 37.8 us
  other arithmetic: 5.12 us -> 0.01 us
    all_gather x2 -> x4, waiting for transfers between devices: 0.02 us -> 183 us  [the longest x2 127 us: spread(): return lax.all_gather(part, 'expert', axis=0, tiled=True)]
    gather x36 -> x2, local copies, waits for them, and re-layouts: 143 us -> 15.7 us  [collect(): mine = everything[flat]]
    all_to_all x2, blocking collectives: 96.8 us -> 24.9 us  [spread(): lax.all_to_all(rows, 'hidden', split_axis=1, concat_axis=0, tiled=True)]
    reduce_scatter x1 -> x2, waiting for transfers between devices: 70.9 us -> 128 us  [the longest x1 83.7 us: local(): own = lax.psum_scatter(sums, 'expert', scatter_dimension=0, tiled=True)]
    all_gather x1 -> x0, blocking collectives: 32.5 us -> none  [local(): all_picks = lax.all_gather(picks, 'expert', axis=0, tiled=True)]
    all_to_all x1, waiting for transfers between devices: 31.9 us -> 0.01 us  [local(): lax.all_to_all(own, 'hidden', split_axis=0, concat_axis=1, tiled=True)]
    scatter x1 -> x0, local copies, waits for them, and re-layouts: 12.4 us -> none  [local(): holder.at[flat_index]]
    select_n x44 -> x1, other arithmetic: 4.53 us -> 0.01 us  [collect(): mine = everything[flat]]
  transfers between devices with their start and end apart: 4 -> 7, of which waited for: 2 -> 6; matrix products, arithmetic and copies ran while one was open for 26% -> 9% of each run, Pallas kernels for 0% -> 0%
where the time goes in v1:
time: 420 us; the launch traced here: 419 us
  waiting for transfers between devices  311 us (74%)
  matrix products  37.8 us (9%)
  blocking collectives  32.8 us (8%)
  local copies, waits for them, and re-layouts  18.8 us (4%)
  between operations  14.2 us (3%)
    all_gather x2, waiting for transfers between devices, spread(): return lax.all_gather(part, 'expert', axis=0, tiled=True)  127 us
    reduce_scatter x1, waiting for transfers between devices, local(): own = lax.psum_scatter(sums, 'expert', scatter_dimension=0, tiled=True)  83.7 us
    all_gather x2, waiting for transfers between devices, collect(): lax.all_gather(mine, 'hidden', axis=1, tiled=True)  56.2 us
    reduce_scatter x1, waiting for transfers between devices, local(): lax.psum_scatter(partial_rows.reshape(exp_local * capacity, width), 'hidd...  44.4 us
    all_to_all x2, blocking collectives, spread(): lax.all_to_all(rows, 'hidden', split_axis=1, concat_axis=0, tiled=True)  24.9 us
    gather x2, local copies, waits for them, and re-layouts, collect(): mine = everything[flat]  15.7 us
  transfers between devices with their start and end apart: 7, of which 6 were waited for; matrix products, arithmetic and copies ran while one was open for 9% of the time, Pallas kernels for 0%

profile of v1, /device:TPU:0, one launch (start us, length us, event | category | flops | bytes accessed | tf_op | source)
XLA Modules:
  0.0 419.1 jit_solution(9010351641995205298)
XLA Ops:
  7.2 1.2 copy.22
  8.4 13.0 %all_to_all.57 = bf16[128,4,512]{2,0,1:T(8,128)(2,1)} all-to-all(bf16[128,4,512]{2,0,1:T(8,128)(2,1)S(1)} %bitcast.54), channel_id=1, replica_groups=mesh['expert'=8,'hidden'=4] {'hidden'}, dimensions={1} | all-to-all | bytes 1048576 | tf_op jit(solution)/shard_map/all_to_all | solution.py:17
  21.5 1.1 copy.23
  22.6 11.9 %all_to_all.58 = bf16[128,4,512]{2,0,1:T(8,128)(2,1)} all-to-all(bf16[128,4,512]{2,0,1:T(8,128)(2,1)S(1)} %bitcast.55), channel_id=1, replica_groups=mesh['expert'=8,'hidden'=4] {'hidden'}, dimensions={1} | all-to-all | bytes 1048576 | tf_op jit(solution)/shard_map/all_to_all | solution.py:17
  34.6 61.1 %all-gather.9.cloned.1.call-done = bf16[4096,512]{1,0:T(8,128)(2,1)} async-done(((bf16[512,512]{1,0:T(8,128)(2,1)}), bf16[4096,512]{1,0:T(8,128)(2,1)}) %all-gather.9.cloned.1.call-update) | async-done | bytes 4194320 | tf_op jit(solution)/shard_map/all_gather | solution.py:18
  95.7 7.8 %gather_fusion.1 = bf16[1024,512]{1,0:T(8,128)(2,1)} fusion(bf16[4096,512]{1,0:T(8,128)(2,1)} %all-gather.9.cloned.1.call-done, s32[1024]{0:T(1024)S(1)} %broadcast_clamp_fusion), kind=kCustom, calls=%fused_computation.1 | custom fusion | bytes 2101248 | tf_op jit(solution)/shard_map/gather | solution.py:21
  103.6 65.9 %all-gather.7.cloned.1.call-done = bf16[4096,512]{1,0:T(8,128)(2,1)} async-done(((bf16[512,512]{1,0:T(8,128)(2,1)}), bf16[4096,512]{1,0:T(8,128)(2,1)}) %all-gather.7.cloned.1.call-update) | async-done | bytes 4194320 | tf_op jit(solution)/shard_map/all_gather | solution.py:18
  169.5 7.8 %gather_fusion = bf16[1024,512]{1,0:T(8,128)(2,1)} fusion(bf16[4096,512]{1,0:T(8,128)(2,1)} %all-gather.7.cloned.1.call-done, s32[1024]{0:T(1024)S(1)} %broadcast_clamp_fusion), kind=kCustom, calls=%fused_computation | custom fusion | bytes 2101248 | tf_op jit(solution)/shard_map/gather | solution.py:21
  177.5 27.0 %all-gather.13.cloned.1.call-done = bf16[1024,2048]{1,0:T(8,128)(2,1)} async-done(((bf16[1024,512]{1,0:T(8,128)(2,1)}), bf16[1024,2048]{1,0:T(8,128)(2,1)}) %all-gather.13.cloned.1.call-update) | async-done | bytes 4194320 | tf_op jit(solution)/shard_map/all_gather | solution.py:22
  204.5 4.8 %fusion.9 = f32[2,512,192]{1,2,0:T(8,128)} fusion(bf16[2,512,2048]{2,1,0:T(8,128)(2,1)} %bitcast.44, bf16[2,192,2048]{2,1,0:T(8,128)(2,1)S(1)} %copy-done), kind=kOutput, calls=%fused_computation.25 | convolution fusion | flops 805306368 | bytes 6553600 | tf_op jit(solution)/shard_map/xcd,xhd->xch/dot_general | solution.py:27
  209.2 2.5 fusion.8
  211.7 29.2 %all-gather.11.cloned.1.call-done = bf16[1024,2048]{1,0:T(8,128)(2,1)} async-done(((bf16[1024,512]{1,0:T(8,128)(2,1)}), bf16[1024,2048]{1,0:T(8,128)(2,1)}) %all-gather.11.cloned.1.call-update) | async-done | bytes 4194320 | tf_op jit(solution)/shard_map/all_gather | solution.py:22
  241.0 5.6 %fusion.3 = (f32[2,512]{1,0:T(2,128)S(1)}, bf16[2,512,192]{1,2,0:T(8,128)(2,1)}, bf16[2,512,192]{1,2,0:T(8,128)(2,1)S(1)}, bf16[2,512,192]{1,2,0:T(8,128)(2,1)S(1)}) fusion(f32[2,512,192]{1,2,0:T(8,128)} %fusion.8, f32[2,512,192]{1,2,0:T(8,128)} %fusion.9, f32[2,512]{1,0:T(2,128)S(1)} %copy-done.6, bf16[2,512,2048]{2,1,0:T(8,128)(2,1)} %bitcast.49, ...), kind=kOutput, calls=%fused_computation.12 | convolution fusion | flops 809040896 | bytes 8527872 | tf_op jit(solution)/shard_map/xcd,xhd->xch/dot_general | solution.py:26
  246.6 1.3 fusion.10
  247.9 3.4 add_convert_fusion
  251.6 44.4 %reduce-scatter.3.cloned.1.call-done = bf16[1024,512]{1,0:T(8,128)(2,1)} async-done(((bf16[1024,2048]{1,0:T(8,128)(2,1)}), bf16[1024,512]{1,0:T(8,128)(2,1)}) %reduce-scatter.3.cloned.1.call-update) | async-done | bytes 1048592 | tf_op jit(solution)/shard_map/reduce_scatter | solution.py:42
  296.0 7.2 %fusion.2 = bf16[4096,512]{1,0:T(8,128)(2,1)} fusion(bf16[1024,512]{1,0:T(8,128)(2,1)} %reduce-scatter.3.cloned.1.call-done, s32[1024]{0:T(1024)S(1)} %bitcast.64), kind=kOutput, calls=%fused_computation.6 | convolution fusion | flops 4301258752 | bytes 5246976 | tf_op jit(solution)/shard_map/dot_general | solution.py:46
  303.2 4.4 %convolution_convert_fusion.2 = bf16[2,192,2048]{2,1,0:T(8,128)(2,1)} fusion(bf16[2,512,192]{1,2,0:T(8,128)(2,1)S(1)} %get-tuple-element.7, bf16[2,512,2048]{2,1,0:T(8,128)(2,1)} %bitcast.45), kind=kOutput, calls=%fused_computation.9 | convolution fusion | flops 806092800 | bytes 6160384 | tf_op jit(solution)/shard_map/xch,xcd->xhd/dot_general | solution.py:52
  307.6 83.7 %reduce-scatter.5.cloned.1.call-done = bf16[512,512]{1,0:T(8,128)(2,1)} async-done(((bf16[4096,512]{1,0:T(8,128)(2,1)}), bf16[512,512]{1,0:T(8,128)(2,1)}) %reduce-scatter.5.cloned.1.call-update) | async-done | bytes 524304 | tf_op jit(solution)/shard_map/reduce_scatter | solution.py:47
  391.3 3.5 all-to-all-start.2
  394.8 4.3 %convolution_convert_fusion.1 = bf16[2,192,2048]{2,1,0:T(8,128)(2,1)} fusion(bf16[2,512,192]{1,2,0:T(8,128)(2,1)S(1)} %copy-done.4, bf16[2,512,2048]{2,1,0:T(8,128)(2,1)} %bitcast.46), kind=kOutput, calls=%fused_computation.8 | convolution fusion | flops 806092800 | bytes 6160384 | tf_op jit(solution)/shard_map/xch,xcd->xhd/dot_general | solution.py:55
  399.1 7.9 %psum.7 = f32[2,512]{1,0:T(2,128)} all-reduce(f32[2,512]{1,0:T(2,128)S(1)} %get-tuple-element.5), channel_id=1, replica_groups=mesh['expert'=8,'hidden'=4] {'hidden'}, use_global_device_ids=true, to_apply=%region_3.0 | all-reduce | flops 1024 | bytes 8192 | tf_op jit(solution)/shard_map/psum | solution.py:33
  407.1 4.3 %convolution_convert_fusion = bf16[2,192,2048]{2,1,0:T(8,128)(2,1)} fusion(bf16[2,512,2048]{2,1,0:T(8,128)(2,1)} %bitcast.50, bf16[2,512,192]{1,2,0:T(8,128)(2,1)S(1)} %copy-done.5, f32[2,512]{1,0:T(2,128)S(1)} %copy-done.6), kind=kOutput, calls=%fused_computation.7 | convolution fusion | flops 806682624 | bytes 6164480 | tf_op jit(solution)/shard_map/xch,xcd->xhd/dot_general | solution.py:49
  411.4 0.9 copy.17
  (33 shorter events, 0.6 us)
Async XLA Ops:
  7.2 197.3 %copy-start = (bf16[2,192,2048]{2,1,0:T(8,128)(2,1)S(1)}, bf16[2,192,2048]{2,1,0:T(8,128)(2,1)}, u32[]{:S(2)}) copy-start(bf16[2,192,2048]{2,1,0:T(8,128)(2,1)} %param.11) | copy-start | bytes 4718596
  7.2 27.4 %copy-start.7 = (s32[2,512]{1,0:T(2,128)S(1)}, s32[2,512]{1,0:T(2,128)}, u32[]{:S(2)}) copy-start(s32[2,512]{1,0:T(2,128)} %param.9) | copy-start | bytes 12292
  7.2 88.5 %all-gather.9.cloned.1.call-start = ((), (), s32[]{:S(2)}) async-start(), calls=%async_computation.6 | async-start | bytes 4718592 | tf_op jit(solution)/shard_map/all_gather | solution.py:18
  21.4 148.1 %all-gather.7.cloned.1.call-start = ((), (), s32[]{:S(2)}) async-start(), calls=%async_computation.5 | async-start | bytes 4718592 | tf_op jit(solution)/shard_map/all_gather | solution.py:18
  34.5 169.9 %all-gather.13.cloned.1.call-start = ((), (), s32[]{:S(2)}) async-start(), calls=%async_computation.10 | async-start | bytes 5242880 | tf_op jit(solution)/shard_map/all_gather | solution.py:22
  103.6 137.4 %all-gather.11.cloned.1.call-start = ((), (), s32[]{:S(2)}) async-start(), calls=%async_computation.9 | async-start | bytes 5242880 | tf_op jit(solution)/shard_map/all_gather | solution.py:22
  177.4 31.8 %copy-start.2 = (bf16[2,192,2048]{2,1,0:T(8,128)(2,1)S(1)}, bf16[2,192,2048]{2,1,0:T(8,128)(2,1)}, u32[]{:S(2)}) copy-start(bf16[2,192,2048]{2,1,0:T(8,128)(2,1)} %param.12) | copy-start | bytes 4718596
  177.4 118.6 %reduce-scatter.3.cloned.1.call-start = ((), (), s32[]{:S(2)}) async-start(), calls=%async_computation.7 | async-start | bytes 5242880 | tf_op jit(solution)/shard_map/reduce_scatter | solution.py:42
  204.5 4.8 %copy-start.1 = (bf16[1024,2048]{1,0:T(8,128)(2,1)S(1)}, bf16[1024,2048]{1,0:T(8,128)(2,1)}, u32[]{:S(2)}) copy-start(bf16[1024,2048]{1,0:T(8,128)(2,1)} %all-gather.13.cloned.1.call-done) | copy-start | bytes 12582916
  209.2 31.7 %copy-start.6 = (f32[2,512]{1,0:T(2,128)S(1)}, f32[2,512]{1,0:T(2,128)}, u32[]{:S(2)}) copy-start(f32[2,512]{1,0:T(2,128)} %param.10) | copy-start | bytes 12292
  246.6 1.3 copy-start.3
  251.3 140.0 %reduce-scatter.5.cloned.1.call-start = ((), (), s32[]{:S(2)}) async-start(), calls=%async_computation.8 | async-start | bytes 4718592 | tf_op jit(solution)/shard_map/reduce_scatter | solution.py:47
  303.2 91.5 %copy-start.4 = (bf16[2,512,192]{1,2,0:T(8,128)(2,1)S(1)}, bf16[2,512,192]{1,2,0:T(8,128)(2,1)}, u32[]{:S(2)}) copy-start(bf16[2,512,192]{1,2,0:T(8,128)(2,1)} %copy-done.3) | copy-start | bytes 1179652
  307.6 99.4 %copy-start.5 = (bf16[2,512,192]{1,2,0:T(8,128)(2,1)S(1)}, bf16[2,512,192]{1,2,0:T(8,128)(2,1)}, u32[]{:S(2)}) copy-start(bf16[2,512,192]{1,2,0:T(8,128)(2,1)} %get-tuple-element.6) | copy-start | bytes 1179652
  391.3 20.1 %all-to-all-start.2 = ((bf16[4,128,512]{2,1,0:T(8,128)(2,1)}), bf16[4,128,512]{2,1,0:T(8,128)(2,1)S(1)}, u32[]{:S(2)}, u32[]{:S(2)}) async-start(bf16[4,128,512]{2,1,0:T(8,128)(2,1)} %bitcast.58), calls=%async_computation.4 | async-start | bytes 1048576 | tf_op jit(solution)/shard_map/all_to_all | solution.py:48
Sparse Core Ops, SparseCore 0:
  21.5 74.1 all-gather.8
  97.8 71.6 all-gather.6
  171.7 32.7 all-gather.12
  206.4 34.4 all-gather.10
  251.4 44.4 reduce-scatter.2
  303.4 87.8 reduce-scatter.4

commit v2 on v1

--- a/solution.py
+++ b/solution.py
@@ -1,7 +1,244 @@
+import functools
 import jax
 import jax.numpy as jnp
 from jax import lax
+from jax.experimental import pallas as pl
+from jax.experimental.pallas import tpu as pltpu
 from jax.sharding import PartitionSpec as P
+
+MESH = pl.DeviceIdType.MESH
+PASSES = 4
+
+
+def dispatch_kernel(
+    nz, tok_ref, grad_ref, picks_ref, out_tok, out_grad, buf, hot,
+    a_send, a_recv, up_send, up_recv, dn_send, dn_recv, y_send, y_recv,
+    x_send, x_recv, c_send, c_recv,
+):
+    e, h = lax.axis_index("expert"), lax.axis_index("hidden")
+    z, y = e // 2, e % 2
+    h_core = h + 1 - 2 * (h % 2)
+    h_x = (h + 2) % 4
+    h_far = (h_core + 2) % 4
+    rows, width = tok_ref.shape
+    cols = width // 4
+    part = buf.shape[-1]
+    halves = cols // part
+    peers = (h_core, h_x, h_far)
+    groups = 2 * nz
+    block = 4 * rows
+
+    barrier = pltpu.get_barrier_semaphore()
+    for peer in peers:
+        pl.semaphore_signal(barrier, inc=1, device_id=(e, peer), device_id_type=MESH)
+    pl.semaphore_signal(barrier, inc=1, device_id=(z * 2 + 1 - y, h), device_id_type=MESH)
+
+    @pl.when(z > 0)
+    def _():
+        pl.semaphore_signal(barrier, inc=1, device_id=(e - 2, h), device_id_type=MESH)
+
+    @pl.when(z < nz - 1)
+    def _():
+        pl.semaphore_signal(barrier, inc=1, device_id=(e + 2, h), device_id_type=MESH)
+
+    ends = jnp.where(z == 0, 1, 0) + jnp.where(z == nz - 1, 1, 0)
+    pl.semaphore_wait(barrier, 6 - ends)
+
+    def source(p):
+        return (tok_ref, grad_ref)[p // halves]
+
+    def output(p):
+        return (out_tok, out_grad)[p // halves]
+
+    def span(p, owner):
+        return pl.ds(pl.multiple_of(owner * cols + (p % halves) * part, part), part)
+
+    def mine(p):
+        return buf.at[p, e, pl.ds(pl.multiple_of(h * rows, rows), rows), :]
+
+    def a_copy(p, d):
+        return pltpu.make_async_remote_copy(
+            src_ref=source(p).at[:, span(p, peers[d])], dst_ref=mine(p),
+            send_sem=a_send.at[p, d], recv_sem=a_recv.at[p, d],
+            device_id=(e, peers[d]), device_id_type=MESH)
+
+    def chunk_copy(p, zz, send, recv, target):
+        ref = buf.at[p, zz * 2 + y]
+        return pltpu.make_async_remote_copy(
+            src_ref=ref, dst_ref=ref, send_sem=send, recv_sem=recv,
+            device_id=(target, h), device_id_type=MESH)
+
+    def up(p, s):
+        return chunk_copy(p, z - (s - 1), up_send.at[p, s - 1], up_recv.at[p, s - 1], e + 2)
+
+    def dn(p, s):
+        return chunk_copy(p, z + (s - 1), dn_send.at[p, s - 1], dn_recv.at[p, s - 1], e - 2)
+
+    def across(p, k, zz):
+        return chunk_copy(p, zz, y_send.at[p, k], y_recv.at[p, k], z * 2 + 1 - y)
+
+    def x_copy(p):
+        ref = output(p).at[:, span(p, h)]
+        return pltpu.make_async_remote_copy(
+            src_ref=ref, dst_ref=ref, send_sem=x_send.at[p], recv_sem=x_recv.at[p],
+            device_id=(e, h_x), device_id_type=MESH)
+
+    def c_copy(p, k):
+        ref = output(p).at[:, span(p, (h, h_x)[k])]
+        return pltpu.make_async_remote_copy(
+            src_ref=ref, dst_ref=ref, send_sem=c_send.at[p, k], recv_sem=c_recv.at[p, k],
+            device_id=(e, h_core), device_id_type=MESH)
+
+    for p in range(PASSES):
+        for d in (1, 2, 0):
+            a_copy(p, d).start()
+        buf[p, e, pl.ds(pl.multiple_of(h * rows, rows), rows), :] = source(p)[:, span(p, h)]
+
+    @pl.loop(0, groups)
+    def _(g):
+        ids = picks_ref[...] - g * block
+        lane = lax.broadcasted_iota(jnp.int32, (ids.shape[0], block), 1)
+        hot[g] = jnp.where(ids == lane, 1.0, 0.0).astype(jnp.bfloat16)
+
+    def own(p):
+        for d in range(3):
+            a_copy(p, d).wait_recv()
+
+        @pl.when(z < nz - 1)
+        def _():
+            up(p, 1).start()
+
+        @pl.when(z > 0)
+        def _():
+            dn(p, 1).start()
+
+        across(p, 0, z).start()
+
+    def step(p, s):
+        @pl.when(z >= s)
+        def _():
+            up(p, s).wait_recv()
+            if s < nz - 1:
+                @pl.when(z < nz - 1)
+                def _():
+                    up(p, s + 1).start()
+            across(p, s, z - s).start()
+
+        @pl.when(z <= nz - 1 - s)
+        def _():
+            dn(p, s).wait_recv()
+            if s < nz - 1:
+                @pl.when(z > 0)
+                def _():
+                    dn(p, s + 1).start()
+            across(p, nz - 1 + s, z + s).start()
+
+    def gathered(p):
+        across(p, 0, z).wait_recv()
+        for s in range(1, nz):
+            @pl.when(z >= s)
+            def _():
+                across(p, s, z - s).wait_recv()
+
+            @pl.when(z <= nz - 1 - s)
+            def _():
+                across(p, nz - 1 + s, z + s).wait_recv()
+
+    def pick(p):
+        step_rows = 256
+        out = output(p)
+
+        @pl.loop(0, out.shape[0] // step_rows)
+        def _(r):
+            here = pl.ds(pl.multiple_of(r * step_rows, step_rows), step_rows)
+            acc = jnp.zeros((step_rows, part), jnp.float32)
+            for g in range(groups):
+                acc += jnp.dot(hot[g, here, :], buf[p, g], preferred_element_type=jnp.float32)
+            out[here, span(p, h)] = acc.astype(jnp.bfloat16)
+
+        x_copy(p).start()
+        c_copy(p, 0).start()
+
+    def forward(p):
+        x_copy(p).wait_recv()
+        c_copy(p, 1).start()
+
+    own(0)
+    own(1)
+    for p in range(PASSES):
+        step(p, 1)
+        if p + 2 < PASSES:
+            own(p + 2)
+        for s in range(2, nz):
+            step(p, s)
+        gathered(p)
+        pick(p)
+        if p > 0:
+            forward(p - 1)
+    forward(PASSES - 1)
+
+    for p in range(PASSES):
+        for d in range(3):
+            a_copy(p, d).wait_send()
+
+        @pl.when(z < nz - 1)
+        def _():
+            up(p, 1).wait_send()
+
+        @pl.when(z > 0)
+        def _():
+            dn(p, 1).wait_send()
+
+        across(p, 0, z).wait_send()
+        for s in range(1, nz):
+            @pl.when(z >= s)
+            def _():
+                if s < nz - 1:
+                    @pl.when(z < nz - 1)
+                    def _():
+                        up(p, s + 1).wait_send()
+                across(p, s, z - s).wait_send()
+
+            @pl.when(z <= nz - 1 - s)
+            def _():
+                if s < nz - 1:
+                    @pl.when(z > 0)
+                    def _():
+                        dn(p, s + 1).wait_send()
+                across(p, nz - 1 + s, z + s).wait_send()
+
+        x_copy(p).wait_send()
+        for k in range(2):
+            c_copy(p, k).wait()
+
+
+def dispatch(tokens, grad_out, picks):
+    groups = lax.axis_size("expert")
+    nz = groups // 2
+    rows, width = tokens.shape
+    total = picks.size
+    part = width // 4 // (PASSES // 2)
+    dma = pltpu.SemaphoreType.DMA
+    out = jax.ShapeDtypeStruct((total, width), jnp.bfloat16)
+    return pl.pallas_call(
+        functools.partial(dispatch_kernel, nz),
+        out_shape=(out, out),
+        in_specs=[pl.BlockSpec(memory_space=pltpu.VMEM)] * 3,
+        out_specs=[pl.BlockSpec(memory_space=pltpu.VMEM)] * 2,
+        scratch_shapes=[
+            pltpu.VMEM((PASSES, groups, 4 * rows, part), jnp.bfloat16),
+            pltpu.VMEM((groups, total, 4 * rows), jnp.bfloat16),
+            dma((PASSES, 3)), dma((PASSES, 3)),
+            dma((PASSES, nz - 1)), dma((PASSES, nz - 1)),
+            dma((PASSES, nz - 1)), dma((PASSES, nz - 1)),
+            dma((PASSES, 2 * nz - 1)), dma((PASSES, 2 * nz - 1)),
+            dma((PASSES,)), dma((PASSES,)),
+            dma((PASSES, 2)), dma((PASSES, 2)),
+        ],
+        compiler_params=pltpu.CompilerParams(
+            collective_id=0, has_side_effects=True, vmem_limit_bytes=48 * 1024 * 1024),
+        name="dispatch",
+    )(tokens, grad_out, picks.reshape(total, 1))
 
 
 def local(tokens, grad_out, picks, gates, w_gate, w_up, w_down):
@@ -21,8 +258,14 @@
         mine = everything[flat]
         return lax.all_gather(mine, "hidden", axis=1, tiled=True).reshape(exp_local, capacity, width)
 
-    picked_grad = collect(spread(grad_out))
-    picked = collect(spread(tokens))
+    fits = shares == 4 and groups % 2 == 0 and total * cols <= 4 * 1024 * 1024
+    if fits:
+        picked, picked_grad = dispatch(tokens, grad_out, picks)
+        picked = picked.reshape(exp_local, capacity, width)
+        picked_grad = picked_grad.reshape(exp_local, capacity, width)
+    else:
+        picked_grad = collect(spread(grad_out))
+        picked = collect(spread(tokens))
     back = jnp.einsum("xcd,xhd->xch", picked_grad, w_down, preferred_element_type=jnp.float32)
     gate = jnp.einsum("xcd,xhd->xch", picked, w_gate, preferred_element_type=jnp.float32)
     up = jnp.einsum("xcd,xhd->xch", picked, w_up, preferred_element_type=jnp.float32)

time: 420 us -> 323 us (0.77)
  waiting for transfers between devices: 311 us -> 130 us
  Pallas kernels: 0 us -> 131 us
  blocking collectives: 32.8 us -> 7.94 us
  local copies, waits for them, and re-layouts: 18.8 us -> 5.53 us
  matrix products: 37.8 us -> 29.8 us
    all_gather x4 -> x0, waiting for transfers between devices: 183 us -> none  [the longest x2 127 us: spread(): return lax.all_gather(part, 'expert', axis=0, tiled=True)]
    pallas_call x0 -> x1, Pallas kernels: none -> 131 us  [dispatch(): pl.pallas_call(functools.partial(dispatch_kernel, nz), out_shape=(out, ou...]
    all_to_all x2 -> x0, blocking collectives: 24.9 us -> none  [spread(): lax.all_to_all(rows, 'hidden', split_axis=1, concat_axis=0, tiled=True)]
    gather x2 -> x0, local copies, waits for them, and re-layouts: 15.7 us -> none  [collect(): mine = everything[flat]]
    unnamed x18 -> x21, local copies, waits for them, and re-layouts: 0.05 us -> 4.68 us
  transfers between devices with their start and end apart: 7 -> 3, of which waited for: 6 -> 2; matrix products, arithmetic and copies ran while one was open for 9% -> 4% of each run, Pallas kernels for 0% -> 0%
where the time goes in v2:
time: 323 us; the launch traced here: 322 us
  Pallas kernels  131 us (41%)
  waiting for transfers between devices  130 us (40%)
  matrix products  29.8 us (9%)
  between operations  14.2 us (4%)
  blocking collectives  7.94 us (2%)
  local copies, waits for them, and re-layouts  5.53 us (2%)
  starting transfers between devices  3.73 us (1%)
    pallas_call x1, Pallas kernels, dispatch(): pl.pallas_call(functools.partial(dispatch_kernel, nz), out_shape=(out, ou...  131 us
    reduce_scatter x1, waiting for transfers between devices, local(): own = lax.psum_scatter(sums, 'expert', scatter_dimension=0, tiled=True)  83.7 us
    reduce_scatter x1, waiting for transfers between devices, local(): lax.psum_scatter(partial_rows.reshape(exp_local * capacity, width), 'hidd...  46 us
    psum x1, blocking collectives, local(): grad_scores = lax.psum(score_part, 'hidden')  7.94 us
    dot_general x1, matrix products, local(): jnp.dot(selector, rows_grad, preferred_element_type=jnp.float32)  7.25 us
  transfers between devices with their start and end apart: 3, of which 2 were waited for; matrix products, arithmetic and copies ran while one was open for 4% of the time, Pallas kernels for 0%

profile of v2, /device:TPU:0, one launch (start us, length us, event | category | flops | bytes accessed | tf_op | source)
XLA Modules:
  0.0 322.2 jit_solution(12443621363212574559)
XLA Ops:
  7.2 0.0 reduce-scatter.3.cloned.1.call-start
  7.2 0.8 copy.17
  8.0 0.2 copy.18
  8.3 1.0 copy-done.2
  9.3 1.0 copy-done.3
  10.4 131.2 %dispatch.1 = (bf16[1024,2048]{1,0:T(8,128)(2,1)S(1)}, bf16[1024,2048]{1,0:T(8,128)(2,1)}) custom-call(bf16[128,2048]{1,0:T(8,128)(2,1)S(1)} %copy-done.2, bf16[128,2048]{1,0:T(8,128)(2,1)S(1)} %copy-done.3, s32[1024,1]{1,0:T(8,128)S(1)} %bitcast.33), custom_call_target="tpu_custom_call" | custom-call | tf_op jit(solution)/shard_map/dispatch/pallas_call | solution.py:223
  141.6 1.5 fusion.9
  143.2 1.5 fusion.8
  144.7 0.6 copy-done.5
  145.4 0.5 copy-done.8
  145.9 1.9 fusion.3
  147.7 1.3 fusion.10
  149.1 3.3 %add_convert_fusion = bf16[2,512,2048]{2,1,0:T(8,128)(2,1)} fusion(f32[2,512,2048]{2,1,0:T(8,128)S(1)} %fusion.10, bf16[2,512,192]{1,2,0:T(8,128)(2,1)S(1)} %get-tuple-element.12, bf16[2,192,2048]{2,1,0:T(8,128)(2,1)S(1)} %copy-done.4), kind=kOutput, calls=%fused_computation.2 | convolution fusion | flops 809500672 | bytes 14548992 | tf_op jit(solution)/shard_map/xch,xhd->xcd/dot_general | solution.py:283
  152.4 0.2 reduce-scatter.5.cloned.1.call-start
  152.6 0.4 copy-done.7
  153.1 46.0 %reduce-scatter.3.cloned.1.call-done = bf16[1024,512]{1,0:T(8,128)(2,1)} async-done(((bf16[1024,2048]{1,0:T(8,128)(2,1)}), bf16[1024,512]{1,0:T(8,128)(2,1)}) %reduce-scatter.3.cloned.1.call-update) | async-done | bytes 1048592 | tf_op jit(solution)/shard_map/reduce_scatter | solution.py:285
  199.1 7.2 %fusion.2 = bf16[4096,512]{1,0:T(8,128)(2,1)} fusion(bf16[1024,512]{1,0:T(8,128)(2,1)} %reduce-scatter.3.cloned.1.call-done, s32[1024]{0:T(1024)S(1)} %bitcast.43), kind=kOutput, calls=%fused_computation.4 | convolution fusion | flops 4301258752 | bytes 5246976 | tf_op jit(solution)/shard_map/dot_general | solution.py:289
  206.4 4.3 %convolution_convert_fusion.2 = bf16[2,192,2048]{2,1,0:T(8,128)(2,1)} fusion(bf16[2,512,192]{1,2,0:T(8,128)(2,1)S(1)} %get-tuple-element.11, bf16[2,512,2048]{2,1,0:T(8,128)(2,1)} %bitcast.31), kind=kOutput, calls=%fused_computation.7 | convolution fusion | flops 806092800 | bytes 6160384 | tf_op jit(solution)/shard_map/xch,xcd->xhd/dot_general | solution.py:295
  210.7 83.7 %reduce-scatter.5.cloned.1.call-done = bf16[512,512]{1,0:T(8,128)(2,1)} async-done(((bf16[4096,512]{1,0:T(8,128)(2,1)}), bf16[512,512]{1,0:T(8,128)(2,1)}) %reduce-scatter.5.cloned.1.call-update) | async-done | bytes 524304 | tf_op jit(solution)/shard_map/reduce_scatter | solution.py:290
  294.4 3.5 %all-to-all-start = ((bf16[4,128,512]{2,1,0:T(8,128)(2,1)}), bf16[4,128,512]{2,1,0:T(8,128)(2,1)S(1)}, u32[]{:S(2)}, u32[]{:S(2)}) async-start(bf16[4,128,512]{2,1,0:T(8,128)(2,1)} %bitcast.38), calls=%async_computation.2 | async-start | bytes 1048576 | tf_op jit(solution)/shard_map/all_to_all | solution.py:291
  297.9 4.3 %convolution_convert_fusion.1 = bf16[2,192,2048]{2,1,0:T(8,128)(2,1)} fusion(bf16[2,512,192]{1,2,0:T(8,128)(2,1)S(1)} %get-tuple-element.12, bf16[2,512,2048]{2,1,0:T(8,128)(2,1)} %bitcast.32), kind=kOutput, calls=%fused_computation.6 | convolution fusion | flops 806092800 | bytes 6160384 | tf_op jit(solution)/shard_map/xch,xcd->xhd/dot_general | solution.py:298
  302.2 7.9 %psum.7 = f32[2,512]{1,0:T(2,128)} all-reduce(f32[2,512]{1,0:T(2,128)S(1)} %get-tuple-element.9), channel_id=1, replica_groups=mesh['expert'=8,'hidden'=4] {'hidden'}, use_global_device_ids=true, to_apply=%region_3.0 | all-reduce | flops 1024 | bytes 8192 | tf_op jit(solution)/shard_map/psum | solution.py:276
  310.2 4.3 %convolution_convert_fusion = bf16[2,192,2048]{2,1,0:T(8,128)(2,1)} fusion(bf16[2,512,2048]{2,1,0:T(8,128)(2,1)} %bitcast.35, bf16[2,512,192]{1,2,0:T(8,128)(2,1)S(1)} %get-tuple-element.10, f32[2,512]{1,0:T(2,128)S(1)} %copy-done.6), kind=kOutput, calls=%fused_computation.5 | convolution fusion | flops 806682624 | bytes 6164480 | tf_op jit(solution)/shard_map/xch,xcd->xhd/dot_general | solution.py:292
  314.5 0.9 copy.15
  (17 shorter events, 0.1 us)
Async XLA Ops:
  7.2 134.5 %copy-start = (bf16[2,192,2048]{2,1,0:T(8,128)(2,1)S(1)}, bf16[2,192,2048]{2,1,0:T(8,128)(2,1)}, u32[]{:S(2)}) copy-start(bf16[2,192,2048]{2,1,0:T(8,128)(2,1)} %param.11) | copy-start | bytes 4718596
  7.2 191.9 %reduce-scatter.3.cloned.1.call-start = ((), (), s32[]{:S(2)}) async-start(), calls=%async_computation.3 | async-start | bytes 5242880 | tf_op jit(solution)/shard_map/reduce_scatter | solution.py:285
  8.3 1.0 copy-start.2
  9.3 1.0 copy-start.3
  10.4 132.8 %copy-start.4 = (bf16[2,192,2048]{2,1,0:T(8,128)(2,1)S(1)}, bf16[2,192,2048]{2,1,0:T(8,128)(2,1)}, u32[]{:S(2)}) copy-start(bf16[2,192,2048]{2,1,0:T(8,128)(2,1)} %param.12) | copy-start | bytes 4718596
  141.6 3.1 copy-start.1
  143.2 2.2 copy-start.5
  143.2 2.2 copy-start.6
  143.2 2.7 copy-start.8
  152.4 0.7 copy-start.7
  152.4 142.0 %reduce-scatter.5.cloned.1.call-start = ((), (), s32[]{:S(2)}) async-start(), calls=%async_computation.4 | async-start | bytes 4718592 | tf_op jit(solution)/shard_map/reduce_scatter | solution.py:290
  294.4 20.1 %all-to-all-start = ((bf16[4,128,512]{2,1,0:T(8,128)(2,1)}), bf16[4,128,512]{2,1,0:T(8,128)(2,1)S(1)}, u32[]{:S(2)}, u32[]{:S(2)}) async-start(bf16[4,128,512]{2,1,0:T(8,128)(2,1)} %bitcast.38), calls=%async_computation.2 | async-start | bytes 1048576 | tf_op jit(solution)/shard_map/all_to_all | solution.py:291
Sparse Core Ops, SparseCore 0:
  152.5 46.5 reduce-scatter.2
  206.5 87.8 reduce-scatter.4

commit v3 on v2

--- a/solution.py
+++ b/solution.py
@@ -241,6 +241,237 @@
     )(tokens, grad_out, picks.reshape(total, 1))
 
 
+BACK = 4
+
+
+def combine_kernel(
+    nz, part_ref, ids_ref, score_ref, out, score_out, near, x_out, x_in, hot, y_out, y_in, keep,
+    dn_out, dn_in, up_out, up_in, fin, scores,
+    a_send, a_recv, x_send, x_recv, y_send, y_recv, dn_send, dn_recv, up_send, up_recv,
+    f_send, f_recv, s_send, s_recv,
+):
+    e, h = lax.axis_index("expert"), lax.axis_index("hidden")
+    z, y = e // 2, e % 2
+    h_core = h + 1 - 2 * (h % 2)
+    h_x = (h + 2) % 4
+    h_far = (h_core + 2) % 4
+    peers = (h_core, h_x, h_far)
+    count, width = part_ref.shape
+    cols = width // 4
+    wide = cols // BACK
+    groups = 2 * nz
+    rows = out.shape[0]
+    block = 4 * rows
+
+    barrier = pltpu.get_barrier_semaphore()
+    for peer in peers:
+        pl.semaphore_signal(barrier, inc=1, device_id=(e, peer), device_id_type=MESH)
+    pl.semaphore_signal(barrier, inc=1, device_id=(z * 2 + 1 - y, h), device_id_type=MESH)
+
+    @pl.when(z > 0)
+    def _():
+        pl.semaphore_signal(barrier, inc=1, device_id=(e - 2, h), device_id_type=MESH)
+
+    @pl.when(z < nz - 1)
+    def _():
+        pl.semaphore_signal(barrier, inc=1, device_id=(e + 2, h), device_id_type=MESH)
+
+    ends = jnp.where(z == 0, 1, 0) + jnp.where(z == nz - 1, 1, 0)
+    pl.semaphore_wait(barrier, 6 - ends)
+
+    def span(q, owner):
+        return pl.ds(pl.multiple_of(owner * cols + q * wide, wide), wide)
+
+    def remote(src, dst, send, recv, target):
+        return pltpu.make_async_remote_copy(
+            src_ref=src, dst_ref=dst, send_sem=send, recv_sem=recv,
+            device_id=target, device_id_type=MESH)
+
+    def a_copy(q, k):
+        return remote(part_ref.at[:, span(q, (h_core, h_far)[k])], near.at[q, k],
+                      a_send.at[q, k], a_recv.at[q, k], (e, h_core))
+
+    def x_copy(q):
+        return remote(x_out.at[q], x_in.at[q], x_send.at[q], x_recv.at[q], (e, h_x))
+
+    def y_copy(q, zz):
+        return remote(y_out.at[q, zz], y_in.at[q, zz], y_send.at[q, zz], y_recv.at[q, zz],
+                      (z * 2 + 1 - y, h))
+
+    def dn_copy(q, j):
+        return remote(dn_out.at[q, j - 1], dn_in.at[q, j - 1], dn_send.at[q, j - 1],
+                      dn_recv.at[q, j - 1], (e - 2, h))
+
+    def up_copy(q, j):
+        return remote(up_out.at[q, j - 1], up_in.at[q, j - 1], up_send.at[q, j - 1],
+                      up_recv.at[q, j - 1], (e + 2, h))
+
+    def f_copy(q, d):
+        return remote(fin.at[q, pl.ds(pl.multiple_of(peers[d] * rows, rows), rows), :],
+                      out.at[:, span(q, h)], f_send.at[q, d], f_recv.at[q, d], (e, peers[d]))
+
+    def s_copy(d):
+        return remote(score_ref, scores.at[h], s_send.at[d], s_recv.at[d], (e, peers[d]))
+
+    for q in range(BACK):
+        a_copy(q, 1).start()
+        a_copy(q, 0).start()
+    for d in range(3):
+        s_copy(d).start()
+    scores[h] = score_ref[...]
+
+    def hidden_send(q):
+        a_copy(q, 1).wait_recv()
+        both = part_ref[:, span(q, h_x)].astype(jnp.float32) + near[q, 1].astype(jnp.float32)
+        x_out[q] = both.astype(jnp.bfloat16)
+        x_copy(q).start()
+
+    def spread_rows(q):
+        a_copy(q, 0).wait_recv()
+        both = part_ref[:, span(q, h)].astype(jnp.float32) + near[q, 0].astype(jnp.float32)
+        x_copy(q).wait_recv()
+        near[q, 0] = (both + x_in[q].astype(jnp.float32)).astype(jnp.bfloat16)
+        for zz in range(nz):
+            y_out[q, zz] = jnp.dot(
+                hot[zz * 2 + 1 - y], near[q, 0], preferred_element_type=jnp.float32
+            ).astype(jnp.bfloat16)
+            y_copy(q, zz).start()
+        for zz in range(nz):
+            keep[q, zz] = jnp.dot(hot[zz * 2 + y], near[q, 0], preferred_element_type=jnp.float32)
+
+    def line(q, j):
+        @pl.when(z >= j)
+        def _():
+            @pl.when(z < nz - 1)
+            def _():
+                if j < nz - 1:
+                    dn_copy(q, j + 1).wait_recv()
+                    keep[q, z - j] += dn_in[q, j].astype(jnp.float32)
+            dn_out[q, j - 1] = keep[q, z - j].astype(jnp.bfloat16)
+            dn_copy(q, j).start()
+
+        @pl.when(z <= nz - 1 - j)
+        def _():
+            @pl.when(z > 0)
+            def _():
+                if j < nz - 1:
+                    up_copy(q, j + 1).wait_recv()
+                    keep[q, z + j] += up_in[q, j].astype(jnp.float32)
+            up_out[q, j - 1] = keep[q, z + j].astype(jnp.bfloat16)
+            up_copy(q, j).start()
+
+    def far(q):
+        for zz in range(nz):
+            y_copy(q, zz).wait_recv()
+            keep[q, zz] += y_in[q, zz].astype(jnp.float32)
+        for j in range(nz - 1, 1, -1):
+            line(q, j)
+
+    def close(q):
+        line(q, 1)
+
+        @pl.when(z < nz - 1)
+        def _():
+            dn_copy(q, 1).wait_recv()
+            keep[q, z] += dn_in[q, 0].astype(jnp.float32)
+
+        @pl.when(z > 0)
+        def _():
+            up_copy(q, 1).wait_recv()
+            keep[q, z] += up_in[q, 0].astype(jnp.float32)
+
+        fin[q] = keep[q, z].astype(jnp.bfloat16)
+        for d in range(3):
+            f_copy(q, d).start()
+        out[:, span(q, h)] = fin[q, pl.ds(pl.multiple_of(h * rows, rows), rows), :]
+
+    hidden_send(0)
+    hidden_send(1)
+
+    @pl.loop(0, groups)
+    def _(g):
+        ids = ids_ref[...] - g * block
+        row = lax.broadcasted_iota(jnp.int32, (block, count), 0)
+        hot[g] = jnp.where(ids == row, 1.0, 0.0).astype(jnp.bfloat16)
+
+    hidden_send(2)
+    hidden_send(3)
+    spread_rows(0)
+    spread_rows(1)
+    far(0)
+    spread_rows(2)
+    close(0)
+    far(1)
+    spread_rows(3)
+    close(1)
+    far(2)
+    close(2)
+    far(3)
+    close(3)
+
+    for d in range(3):
+        s_copy(d).wait()
+    score_out[...] = scores[0] + scores[1] + scores[2] + scores[3]
+
+    for q in range(BACK):
+        for k in range(2):
+            a_copy(q, k).wait_send()
+        x_copy(q).wait_send()
+        for zz in range(nz):
+            y_copy(q, zz).wait_send()
+        for j in range(1, nz):
+            @pl.when(z >= j)
+            def _():
+                dn_copy(q, j).wait_send()
+
+            @pl.when(z <= nz - 1 - j)
+            def _():
+                up_copy(q, j).wait_send()
+        for d in range(3):
+            f_copy(q, d).wait()
+
+
+def combine(partial_rows, picks, score_part, rows):
+    groups = lax.axis_size("expert")
+    nz = groups // 2
+    count, width = partial_rows.shape
+    wide = width // 4 // BACK
+    block = 4 * rows
+    dma = pltpu.SemaphoreType.DMA
+    low = jnp.bfloat16
+    vmem = pl.BlockSpec(memory_space=pltpu.VMEM)
+    line = pltpu.VMEM((BACK, nz - 1, block, wide), low)
+    out, scores = pl.pallas_call(
+        functools.partial(combine_kernel, nz),
+        out_shape=(
+            jax.ShapeDtypeStruct((rows, width), low),
+            jax.ShapeDtypeStruct((count // 128, 128), jnp.float32),
+        ),
+        in_specs=[vmem] * 3,
+        out_specs=[vmem] * 2,
+        scratch_shapes=[
+            pltpu.VMEM((BACK, 2, count, wide), low),
+            pltpu.VMEM((BACK, count, wide), low),
+            pltpu.VMEM((BACK, count, wide), low),
+            pltpu.VMEM((groups, block, count), low),
+            pltpu.VMEM((BACK, nz, block, wide), low),
+            pltpu.VMEM((BACK, nz, block, wide), low),
+            pltpu.VMEM((BACK, nz, block, wide), jnp.float32),
+            line, line, line, line,
+            pltpu.VMEM((BACK, block, wide), low),
+            pltpu.VMEM((4, count // 128, 128), jnp.float32),
+            dma((BACK, 2)), dma((BACK, 2)), dma((BACK,)), dma((BACK,)),
+            dma((BACK, nz)), dma((BACK, nz)),
+            dma((BACK, nz - 1)), dma((BACK, nz - 1)), dma((BACK, nz - 1)), dma((BACK, nz - 1)),
+            dma((BACK, 3)), dma((BACK, 3)), dma((3,)), dma((3,)),
+        ],
+        compiler_params=pltpu.CompilerParams(
+            collective_id=1, has_side_effects=True, vmem_limit_bytes=48 * 1024 * 1024),
+        name="combine",
+    )(partial_rows, picks.reshape(1, count), score_part.reshape(count // 128, 128))
+    return out, scores.reshape(score_part.shape)
+
+
 def local(tokens, grad_out, picks, gates, w_gate, w_up, w_down):
     groups = lax.axis_size("expert")
     shares = lax.axis_size("hidden")
@@ -273,7 +504,6 @@
     act = gate * sig
     hid = (act * up).astype(jnp.bfloat16)
     score_part = jnp.sum(hid.astype(jnp.float32) * back, axis=-1)
-    grad_scores = lax.psum(score_part, "hidden")
     grad_hid = gates[:, :, None] * back
     grad_gate = (grad_hid * up * sig * (1.0 + gate * (1.0 - sig))).astype(jnp.bfloat16)
     grad_up = (grad_hid * act).astype(jnp.bfloat16)
@@ -282,13 +512,19 @@
         jnp.einsum("xch,xhd->xcd", grad_gate, w_gate, preferred_element_type=jnp.float32)
         + jnp.einsum("xch,xhd->xcd", grad_up, w_up, preferred_element_type=jnp.float32)
     ).astype(jnp.bfloat16)
-    rows_grad = lax.psum_scatter(
-        partial_rows.reshape(exp_local * capacity, width), "hidden", scatter_dimension=1, tiled=True
-    )
-    selector = (jnp.arange(total, dtype=jnp.int32)[:, None] == flat[None, :]).astype(jnp.bfloat16)
-    sums = jnp.dot(selector, rows_grad, preferred_element_type=jnp.float32).astype(jnp.bfloat16)
-    own = lax.psum_scatter(sums, "expert", scatter_dimension=0, tiled=True)
-    grad_tokens = lax.all_to_all(own, "hidden", split_axis=0, concat_axis=1, tiled=True)
+    if fits:
+        grad_tokens, grad_scores = combine(
+            partial_rows.reshape(exp_local * capacity, width), picks, score_part, tok_rows
+        )
+    else:
+        grad_scores = lax.psum(score_part, "hidden")
+        rows_grad = lax.psum_scatter(
+            partial_rows.reshape(exp_local * capacity, width), "hidden", scatter_dimension=1, tiled=True
+        )
+        selector = (jnp.arange(total, dtype=jnp.int32)[:, None] == flat[None, :]).astype(jnp.bfloat16)
+        sums = jnp.dot(selector, rows_grad, preferred_element_type=jnp.float32).astype(jnp.bfloat16)
+        own = lax.psum_scatter(sums, "expert", scatter_dimension=0, tiled=True)
+        grad_tokens = lax.all_to_all(own, "hidden", split_axis=0, concat_axis=1, tiled=True)
     grad_w_down = jnp.einsum(
         "xch,xcd->xhd", weighted, picked_grad, preferred_element_type=jnp.float32
     ).astype(jnp.bfloat16)

time: 323 us -> 237 us (0.73)
  waiting for transfers between devices: 130 us -> 0 us
  Pallas kernels: 131 us -> 214 us
  matrix products: 29.8 us -> 16.3 us
  between operations: 14.2 us -> 0.75 us
  blocking collectives: 7.94 us -> 0 us
  starting transfers between devices: 3.73 us -> 0 us
    reduce_scatter x2 -> x0, waiting for transfers between devices: 130 us -> none  [the longest x1 83.7 us: local(): own = lax.psum_scatter(sums, 'expert', scatter_dimension=0, tiled=True)]
    pallas_call x0 -> x1, Pallas kernels: none -> 82.6 us  [combine(): pl.pallas_call(functools.partial(combine_kernel, nz), out_shape=(jax.Shap...]
    psum x1 -> x0, blocking collectives: 7.94 us -> none  [local(): grad_scores = lax.psum(score_part, 'hidden')]
    dot_general x1 -> x0, matrix products: 7.25 us -> none  [local(): jnp.dot(selector, rows_grad, preferred_element_type=jnp.float32)]
    all_to_all x1 -> x0, starting transfers between devices: 3.47 us -> none  [local(): lax.all_to_all(own, 'hidden', split_axis=0, concat_axis=1, tiled=True)]
  transfers between devices with their start and end apart: 3 -> 0, of which waited for: 2 -> 0; matrix products, arithmetic and copies ran while one was open for 4% -> 0% of each run, Pallas kernels for 0% -> 0%
where the time goes in v3:
time: 237 us
  Pallas kernels  214 us (90%)
  matrix products  16.3 us (7%)
  local copies, waits for them, and re-layouts  5.76 us (2%)
    pallas_call x1, Pallas kernels, dispatch(): pl.pallas_call(functools.partial(dispatch_kernel, nz), out_shape=(out, ou...  131 us
    pallas_call x1, Pallas kernels, combine(): pl.pallas_call(functools.partial(combine_kernel, nz), out_shape=(jax.Shap...  82.6 us
    unnamed x23, local copies, waits for them, and re-layouts  5.15 us

profile of v3, /device:TPU:0, one launch (start us, length us, event | category | flops | bytes accessed | tf_op | source)
XLA Modules:
  0.0 236.7 jit_solution(1344787369422128228)
XLA Ops:
  0.6 0.0 copy-start
  0.6 0.8 copy.13
  1.5 0.2 copy.14
  1.7 0.0 copy-start.3
  1.7 1.0 copy-done.3
  2.7 1.0 copy-done.4
  3.8 131.3 %dispatch.1 = (bf16[1024,2048]{1,0:T(8,128)(2,1)S(1)}, bf16[1024,2048]{1,0:T(8,128)(2,1)}) custom-call(bf16[128,2048]{1,0:T(8,128)(2,1)S(1)} %copy-done.3, bf16[128,2048]{1,0:T(8,128)(2,1)S(1)} %copy-done.4, s32[1024,1]{1,0:T(8,128)S(1)} %bitcast.30), custom_call_target="tpu_custom_call" | custom-call | tf_op jit(solution)/shard_map/dispatch/pallas_call | solution.py:223
  135.1 1.5 fusion.6
  136.6 0.0 copy-start.8
  136.6 0.0 copy-start.9
  136.6 1.5 fusion.5
  138.2 0.0 copy-done.1
  138.2 0.6 copy-done.7
  138.8 0.5 copy-done.9
  139.3 1.8 fusion
  141.1 2.1 convolution_convert_fusion
  143.3 4.5 %convolution_convert_fusion.2 = bf16[2,192,2048]{2,1,0:T(8,128)(2,1)} fusion(bf16[2,512,192]{1,2,0:T(8,128)(2,1)S(1)} %get-tuple-element.15, bf16[2,512,2048]{2,1,0:T(8,128)(2,1)} %bitcast.27), kind=kOutput, calls=%fused_computation.3 | convolution fusion | flops 806092800 | bytes 6160384 | tf_op jit(solution)/shard_map/xch,xcd->xhd/dot_general | solution.py:531
  147.8 2.1 convolution_convert_fusion.1
  149.9 1.3 fusion.7
  151.2 0.1 copy-done.6
  151.3 1.4 add_convert_fusion
  152.7 82.6 %combine.1 = (bf16[128,2048]{1,0:T(8,128)(2,1)S(1)}, f32[8,128]{1,0:T(8,128)S(1)}) custom-call(bf16[1024,2048]{1,0:T(8,128)(2,1)S(1)} %bitcast.29, s32[1,1024]{1,0:T(1,128)S(1)} %bitcast.32, f32[8,128]{1,0:T(8,128)S(1)} %reshape.37.score_ref), custom_call_target="tpu_custom_call" | custom-call | tf_op jit(solution)/shard_map/combine/pallas_call | solution.py:444
  235.3 0.6 reshape.38
  235.9 0.8 copy.17
  (11 shorter events, 0.0 us)
Async XLA Ops:
  0.6 134.4 %copy-start = (bf16[2,192,2048]{2,1,0:T(8,128)(2,1)S(1)}, bf16[2,192,2048]{2,1,0:T(8,128)(2,1)}, u32[]{:S(2)}) copy-start(bf16[2,192,2048]{2,1,0:T(8,128)(2,1)} %param.11) | copy-start | bytes 4718596
  1.7 1.0 copy-start.3
  2.7 1.0 copy-start.4
  3.8 132.8 %copy-start.5 = (bf16[2,192,2048]{2,1,0:T(8,128)(2,1)S(1)}, bf16[2,192,2048]{2,1,0:T(8,128)(2,1)}, u32[]{:S(2)}) copy-start(bf16[2,192,2048]{2,1,0:T(8,128)(2,1)} %param.12) | copy-start | bytes 4718596
  135.0 3.1 %copy-start.1 = (bf16[1024,2048]{1,0:T(8,128)(2,1)}, bf16[1024,2048]{1,0:T(8,128)(2,1)S(1)}, u32[]{:S(2)}) copy-start(bf16[1024,2048]{1,0:T(8,128)(2,1)S(1)} %get-tuple-element.10) | copy-start | bytes 12582916
  136.6 2.2 copy-start.7
  136.6 2.2 copy-start.8
  136.6 2.7 %copy-start.9 = (bf16[2,192,2048]{2,1,0:T(8,128)(2,1)S(1)}, bf16[2,192,2048]{2,1,0:T(8,128)(2,1)}, u32[]{:S(2)}) copy-start(bf16[2,192,2048]{2,1,0:T(8,128)(2,1)} %param.13) | copy-start | bytes 4718596
  143.3 4.5 %copy-start.2 = (bf16[1024,2048]{1,0:T(8,128)(2,1)S(1)}, bf16[1024,2048]{1,0:T(8,128)(2,1)}, u32[]{:S(2)}) copy-start(bf16[1024,2048]{1,0:T(8,128)(2,1)} %copy-done.1) | copy-start | bytes 12582916
  149.9 1.4 copy-start.6

commit v4 on v3

--- a/solution.py
+++ b/solution.py
@@ -13,7 +13,7 @@
 def dispatch_kernel(
     nz, tok_ref, grad_ref, picks_ref, out_tok, out_grad, buf, hot,
     a_send, a_recv, up_send, up_recv, dn_send, dn_recv, y_send, y_recv,
-    x_send, x_recv, c_send, c_recv,
+    x_send, x_recv, c_send, c_recv, e_send, e_recv,
 ):
     e, h = lax.axis_index("expert"), lax.axis_index("hidden")
     z, y = e // 2, e % 2
@@ -77,6 +77,58 @@
     def across(p, k, zz):
         return chunk_copy(p, zz, y_send.at[p, k], y_recv.at[p, k], z * 2 + 1 - y)
 
+    def part_copy(p, group, first, send, recv, target):
+        ref = buf.at[p, group, pl.ds(first, block // 2), :]
+        return pltpu.make_async_remote_copy(
+            src_ref=ref, dst_ref=ref, send_sem=send, recv_sem=recv,
+            device_id=(target, h), device_id_type=MESH)
+
+    def across_half(p, k, zz):
+        return part_copy(p, zz * 2 + y, 0, y_send.at[p, k], y_recv.at[p, k], z * 2 + 1 - y)
+
+    def extra(p, zz, target):
+        return part_copy(p, zz * 2 + 1 - y, block // 2, e_send.at[p], e_recv.at[p], target)
+
+    def across_do(p, s, act):
+        at_top, at_low = z == nz - 1, z == 0
+
+        @pl.when(z >= s)
+        def _():
+            if s > 1:
+                act(across(p, s, z - s))
+            else:
+                @pl.when(at_top)
+                def _():
+                    act(across_half(p, s, z - s))
+
+                @pl.when(z < nz - 1)
+                def _():
+                    act(across(p, s, z - s))
+
+        @pl.when(z <= nz - 1 - s)
+        def _():
+            if s > 1:
+                act(across(p, nz - 1 + s, z + s))
+            else:
+                @pl.when(at_low)
+                def _():
+                    act(across_half(p, nz - 1 + s, z + s))
+
+                @pl.when(z > 0)
+                def _():
+                    act(across(p, nz - 1 + s, z + s))
+
+    def relay(p):
+        across(p, 0, z).wait_recv()
+
+        @pl.when(z == 1)
+        def _():
+            extra(p, z, e - 2).start()
+
+        @pl.when(z == nz - 2)
+        def _():
+            extra(p, z, e + 2).start()
+
     def x_copy(p):
         ref = output(p).at[:, span(p, h)]
         return pltpu.make_async_remote_copy(
@@ -122,7 +174,6 @@
                 @pl.when(z < nz - 1)
                 def _():
                     up(p, s + 1).start()
-            across(p, s, z - s).start()
 
         @pl.when(z <= nz - 1 - s)
         def _():
@@ -131,18 +182,20 @@
                 @pl.when(z > 0)
                 def _():
                     dn(p, s + 1).start()
-            across(p, nz - 1 + s, z + s).start()
+
+        across_do(p, s, lambda copy: copy.start())
 
     def gathered(p):
-        across(p, 0, z).wait_recv()
         for s in range(1, nz):
-            @pl.when(z >= s)
-            def _():
-                across(p, s, z - s).wait_recv()
-
-            @pl.when(z <= nz - 1 - s)
-            def _():
-                across(p, nz - 1 + s, z + s).wait_recv()
+            across_do(p, s, lambda copy: copy.wait_recv())
+
+        @pl.when(z == 0)
+        def _():
+            extra(p, 1, e).wait_recv()
+
+        @pl.when(z == nz - 1)
+        def _():
+            extra(p, nz - 2, e).wait_recv()
 
     def pick(p):
         step_rows = 256
@@ -169,6 +222,7 @@
         step(p, 1)
         if p + 2 < PASSES:
             own(p + 2)
+        relay(p)
         for s in range(2, nz):
             step(p, s)
         gathered(p)
@@ -197,7 +251,6 @@
                     @pl.when(z < nz - 1)
                     def _():
                         up(p, s + 1).wait_send()
-                across(p, s, z - s).wait_send()
 
             @pl.when(z <= nz - 1 - s)
             def _():
@@ -205,7 +258,11 @@
                     @pl.when(z > 0)
                     def _():
                         dn(p, s + 1).wait_send()
-                across(p, nz - 1 + s, z + s).wait_send()
+            across_do(p, s, lambda copy: copy.wait_send())
+
+        @pl.when((z == 1) | (z == nz - 2))
+        def _():
+            extra(p, z, e).wait_send()
 
         x_copy(p).wait_send()
         for k in range(2):
@@ -234,6 +291,7 @@
             dma((PASSES, 2 * nz - 1)), dma((PASSES, 2 * nz - 1)),
             dma((PASSES,)), dma((PASSES,)),
             dma((PASSES, 2)), dma((PASSES, 2)),
+            dma((PASSES,)), dma((PASSES,)),
         ],
         compiler_params=pltpu.CompilerParams(
             collective_id=0, has_side_effects=True, vmem_limit_bytes=48 * 1024 * 1024),
@@ -489,7 +547,7 @@
         mine = everything[flat]
         return lax.all_gather(mine, "hidden", axis=1, tiled=True).reshape(exp_local, capacity, width)
 
-    fits = shares == 4 and groups % 2 == 0 and total * cols <= 4 * 1024 * 1024
+    fits = shares == 4 and groups % 2 == 0 and groups == 8 and total * cols <= 4 * 1024 * 1024
     if fits:
         picked, picked_grad = dispatch(tokens, grad_out, picks)
         picked = picked.reshape(exp_local, capacity, width)

time: 237 us -> 240 us (1.013)
  Pallas kernels: 214 us -> 217 us
    pallas_call x1, Pallas kernels: 131 us -> 134 us  [dispatch(): pl.pallas_call(functools.partial(dispatch_kernel, nz), out_shape=(out, ou...]
where the time goes in v4:
time: 240 us
  Pallas kernels  217 us (90%)
  matrix products  16.3 us (7%)
  local copies, waits for them, and re-layouts  5.76 us (2%)
    pallas_call x1, Pallas kernels, dispatch(): pl.pallas_call(functools.partial(dispatch_kernel, nz), out_shape=(out, ou...  134 us
    pallas_call x1, Pallas kernels, combine(): pl.pallas_call(functools.partial(combine_kernel, nz), out_shape=(jax.Shap...  82.6 us
    unnamed x23, local copies, waits for them, and re-layouts  5.15 us

profile of v4, /device:TPU:0, one launch (start us, length us, event | category | flops | bytes accessed | tf_op | source)
XLA Modules:
  0.0 239.8 jit_solution(9805775824807196008)
XLA Ops:
  0.6 0.0 copy-start
  0.6 0.8 copy.13
  1.5 0.2 copy.14
  1.7 0.0 copy-start.3
  1.7 1.0 copy-done.3
  2.7 1.0 copy-done.4
  3.8 134.4 %dispatch.1 = (bf16[1024,2048]{1,0:T(8,128)(2,1)S(1)}, bf16[1024,2048]{1,0:T(8,128)(2,1)}) custom-call(bf16[128,2048]{1,0:T(8,128)(2,1)S(1)} %copy-done.3, bf16[128,2048]{1,0:T(8,128)(2,1)S(1)} %copy-done.4, s32[1024,1]{1,0:T(8,128)S(1)} %bitcast.30), custom_call_target="tpu_custom_call" | custom-call | tf_op jit(solution)/shard_map/dispatch/pallas_call | solution.py:280
  138.1 0.0 copy-start.1
  138.2 1.5 fusion.6
  139.7 0.0 copy-start.8
  139.7 0.0 copy-start.9
  139.7 1.5 fusion.5
  141.3 0.6 copy-done.7
  141.9 0.5 copy-done.9
  142.4 1.8 fusion
  144.2 2.1 convolution_convert_fusion
  146.4 4.5 %convolution_convert_fusion.2 = bf16[2,192,2048]{2,1,0:T(8,128)(2,1)} fusion(bf16[2,512,192]{1,2,0:T(8,128)(2,1)S(1)} %get-tuple-element.15, bf16[2,512,2048]{2,1,0:T(8,128)(2,1)} %bitcast.27), kind=kOutput, calls=%fused_computation.3 | convolution fusion | flops 806092800 | bytes 6160384 | tf_op jit(solution)/shard_map/xch,xcd->xhd/dot_general | solution.py:589
  150.9 2.1 convolution_convert_fusion.1
  153.0 1.3 fusion.7
  154.3 0.1 copy-done.6
  154.4 1.4 add_convert_fusion
  155.8 82.6 %combine.1 = (bf16[128,2048]{1,0:T(8,128)(2,1)S(1)}, f32[8,128]{1,0:T(8,128)S(1)}) custom-call(bf16[1024,2048]{1,0:T(8,128)(2,1)S(1)} %bitcast.29, s32[1,1024]{1,0:T(1,128)S(1)} %bitcast.32, f32[8,128]{1,0:T(8,128)S(1)} %reshape.37.score_ref), custom_call_target="tpu_custom_call" | custom-call | tf_op jit(solution)/shard_map/combine/pallas_call | solution.py:502
  238.4 0.6 reshape.38
  239.0 0.8 copy.17
  (11 shorter events, 0.0 us)
Async XLA Ops:
  0.6 137.5 %copy-start = (bf16[2,192,2048]{2,1,0:T(8,128)(2,1)S(1)}, bf16[2,192,2048]{2,1,0:T(8,128)(2,1)}, u32[]{:S(2)}) copy-start(bf16[2,192,2048]{2,1,0:T(8,128)(2,1)} %param.11) | copy-start | bytes 4718596
  1.7 1.0 copy-start.3
  2.7 1.0 copy-start.4
  3.8 135.9 %copy-start.5 = (bf16[2,192,2048]{2,1,0:T(8,128)(2,1)S(1)}, bf16[2,192,2048]{2,1,0:T(8,128)(2,1)}, u32[]{:S(2)}) copy-start(bf16[2,192,2048]{2,1,0:T(8,128)(2,1)} %param.12) | copy-start | bytes 4718596
  138.1 3.1 %copy-start.1 = (bf16[1024,2048]{1,0:T(8,128)(2,1)}, bf16[1024,2048]{1,0:T(8,128)(2,1)S(1)}, u32[]{:S(2)}) copy-start(bf16[1024,2048]{1,0:T(8,128)(2,1)S(1)} %get-tuple-element.10) | copy-start | bytes 12582916
  139.7 2.2 copy-start.7
  139.7 2.2 copy-start.8
  139.7 2.7 %copy-start.9 = (bf16[2,192,2048]{2,1,0:T(8,128)(2,1)S(1)}, bf16[2,192,2048]{2,1,0:T(8,128)(2,1)}, u32[]{:S(2)}) copy-start(bf16[2,192,2048]{2,1,0:T(8,128)(2,1)} %param.13) | copy-start | bytes 4718596
  146.4 4.5 %copy-start.2 = (bf16[1024,2048]{1,0:T(8,128)(2,1)S(1)}, bf16[1024,2048]{1,0:T(8,128)(2,1)}, u32[]{:S(2)}) copy-start(bf16[1024,2048]{1,0:T(8,128)(2,1)} %copy-done.1) | copy-start | bytes 12582916
  153.0 1.4 copy-start.6
